TPU v7x, 32 devices: a whole 2x2x4 slice. The times are simulated.
32 devices in a mesh: dp: 8 (over y, x, core), head: 4 (over z).
Axes of the slice: x: 2, y: 2, z: 4, core: 2. Of those that a mesh axis runs over, the one named last changes fastest.
Arguments:
- tile_features: bfloat16 [16, 1601, 7680], P('dp', None, 'head'), may hold values from -6 to 6
- projection: bfloat16 [7680, 8, 256], P('head'), may hold values from -0.09375 to 0.09375
- queries: bfloat16 [8, 64, 8192], P('dp', None, 'head'), may hold values from -36 to 36
- query_gain: float32 [128], replicated, may hold values from 1 to 2.2
- key_gain: float32 [128], replicated, may hold values from 1 to 2.2
- tile_count: int32 [8], P('dp'), may hold values from 1 to 4, as said below
- tile_slot: int32 [8, 4], P('dp'), may hold values from 0 to 15, as said below
- cross_mask: int32 [8, 64, 4], P('dp'), may hold values 0 or 1
- prompt_length: int32 [8], P('dp'), may hold values from 16 to 64, as said below
Outputs:
- context: bfloat16 [8, 64, 8192], P('dp', None, 'head')
Inputs may be any that keep to these rules, and one draw needn't show every extreme that they name: `tile_count`: the counts of each aligned group of 4 requests sum to 8; some request has 4 tiles and some has one. Slot s sits on index s // 2 of dp; every slot holds exactly one tile; for t < tile_count[r], tile_slot[r, t] is the slot of tile t of request r, one of the 8 slots of the aligned group of 4 indices of dp that holds request r; entries with t >= tile_count[r] are arbitrary slots. `prompt_length`: some request uses all 64 rows.
All inputs are finite; a program needn't handle non-finite values. No bound on the sum of `cross_mask` on one device may be relied on, other than what follows from the above.
Results may differ from a plain program's by a relative error of at most 0.04.
Values may be sent and summed in bfloat16 or wider, within the bound.
A program may use at most 128 MiB of HBM per device.

v0:
```python
import math

import jax
import jax.numpy as jnp
from jax import lax
from jax.sharding import PartitionSpec as P

HEADS = 64
KVH = 8
HD = 128
MAXT = 4
GROUP = 4


def swapped(array, axis, distance):
    return lax.ppermute(array, axis, [(i, i ^ 1 << distance) for i in range(lax.axis_size(axis))])


def normalize_rows(values, row_gain):
    squares = jnp.mean(values * values, axis=-1, keepdims=True)
    return values * lax.rsqrt(squares + 1e-05) * row_gain


def attend_tile(query_block, tile_block, usable):
    key_tile = tile_block[..., :HD]
    value_tile = tile_block[..., HD:]
    scores = jnp.einsum(
        "kgpd,knd->kgpn", query_block, key_tile, preferred_element_type=jnp.float32
    ) * (1.0 / math.sqrt(HD))
    weights = jnp.where(usable[None, None, :, None], jnp.exp(scores), 0.0).astype(jnp.bfloat16)
    denominator = jnp.sum(weights, axis=-1, dtype=jnp.float32)
    numerator = jnp.einsum(
        "kgpn,knd->kgpd", weights, value_tile, preferred_element_type=jnp.float32
    )
    return (numerator, denominator)


def order_pair(upper_half, own_part, peer_part):
    return jnp.concatenate(
        [jnp.where(upper_half, peer_part, own_part), jnp.where(upper_half, own_part, peer_part)],
        axis=0,
    )


def local(
    tile_features,
    projection,
    queries,
    query_gain,
    key_gain,
    tile_count,
    tile_slot,
    cross_mask,
    prompt_length,
):
    slots_here, tile_rows, width_here = tile_features.shape
    key_heads = projection.shape[1] // lax.axis_size("head")
    group_size = HEADS // KVH
    prompt_rows = queries.shape[1]
    flat_rows = tile_features.reshape(slots_here * tile_rows, width_here)
    summed = lax.psum_scatter(
        jnp.einsum("rw,wkc->krc", flat_rows, projection, preferred_element_type=jnp.float32).astype(
            jnp.bfloat16
        ),
        "head",
        scatter_dimension=0,
        tiled=True,
    )
    kv_tiles = summed.reshape(key_heads, slots_here, tile_rows, 2 * HD)
    keys_normed = normalize_rows(kv_tiles[..., :HD].astype(jnp.float32), key_gain).astype(
        jnp.bfloat16
    )
    prepared = jnp.concatenate([keys_normed, kv_tiles[..., HD:]], axis=-1)
    query_heads = queries[0].reshape(prompt_rows, key_heads, group_size, HD)
    query_block = normalize_rows(query_heads.astype(jnp.float32), query_gain).astype(jnp.bfloat16)
    query_block = query_block.transpose(1, 2, 0, 3)
    row_index = jnp.arange(prompt_rows, dtype=jnp.int32)
    tile_range = jnp.arange(MAXT, dtype=jnp.int32)
    own_count = tile_count[0]
    own_slots = tile_slot[0]
    own_mask = cross_mask[0]
    own_length = prompt_length[0]
    own_index = lax.axis_index("dp")
    bit_count = GROUP.bit_length() - 1
    numerator = jnp.zeros((key_heads, group_size, prompt_rows, HD), jnp.float32)
    denominator = jnp.zeros((key_heads, group_size, prompt_rows), jnp.float32)
    shared = prepared.transpose(1, 0, 2, 3)
    for bit_level in range(bit_count):
        partner = swapped(shared, "dp", bit_level)
        upper_half = own_index >> bit_level & 1 == 1
        shared = order_pair(upper_half, shared, partner)
    group_base = (own_index - own_index % GROUP) * slots_here
    for tile_pos in range(MAXT):
        tile_block = lax.dynamic_index_in_dim(
            shared, own_slots[tile_pos] - group_base, 0, keepdims=False
        )
        usable = (own_mask[:, tile_pos] == 1) & (tile_pos < own_count) & (row_index < own_length)
        numer_tile, denom_tile = attend_tile(query_block, tile_block, usable)
        numerator = numerator + numer_tile
        denominator = denominator + denom_tile
    live_rows = (row_index < own_length) & jnp.any(
        (own_mask == 1) & (tile_range[None, :] < own_count), axis=1
    )
    divisor = jnp.where(live_rows[None, None, :], denominator, 1.0)
    result = jnp.where(live_rows[None, None, :, None], numerator / divisor[..., None], 0.0)
    context = result.transpose(2, 0, 1, 3).reshape(1, prompt_rows, key_heads * group_size * HD)
    return context.astype(jnp.bfloat16)


def solution(mesh):
    in_specs = (
        P("dp", None, "head"),
        P("head", None, None),
        P("dp", None, "head"),
        P(),
        P(),
        P("dp"),
        P("dp", None),
        P("dp", None, None),
        P("dp"),
    )
    out_specs = P("dp", None, "head")
    return jax.shard_map(local, mesh=mesh, in_specs=in_specs, out_specs=out_specs, check_vma=False)
```

profile of v0, /device:TPU:0, one launch (start us, length us, event | category | flops | bytes accessed | tf_op | source)
XLA Modules:
  0.0 523.2 jit_solution(420937420121785636)
XLA Ops:
  6.5 11.9 %copy.31 = bf16[2,1601,1920]{2,1,0:T(8,128)(2,1)} copy(bf16[2,1601,1920]{2,0,1:T(2,128)(2,1)} %param.9) | data formatting | bytes 24591360 | tf_op args[0]
  18.4 11.3 %reshape.134 = bf16[3202,1920,1]{1,0,2:T(8,128)(2,1)} reshape(bf16[2,1601,1920]{2,1,0:T(8,128)(2,1)} %copy.31) | data formatting | bytes 24591360 | tf_op jit(solution)/shard_map/reshape | solution.py:60
  29.7 34.6 %convert_bitcast_fusion = bf16[8,3202,256]{2,1,0:T(8,128)(2,1)} fusion(bf16[3202,1920,1]{1,0,2:T(8,128)(2,1)} %reshape.134, bf16[1920,8,256]{2,1,0:T(8,128)(2,1)} %param.10), kind=kOutput, calls=%fused_computation.8 | convolution fusion | flops 25188110336 | bytes 33275392 | tf_op jit(solution)/shard_map/rw,wkc->krc/dot_general | solution.py:62
  64.3 224.0 %reduce-scatter.2.cloned.1.call-done = bf16[2,3202,256]{2,1,0:T(8,128)(2,1)} async-done(((bf16[8,3202,256]{2,1,0:T(8,128)(2,1)}), bf16[2,3202,256]{2,1,0:T(8,128)(2,1)}) %reduce-scatter.2.cloned.1.call-update) | async-done | bytes 3278864 | tf_op jit(solution)/shard_map/reduce_scatter | solution.py:61
  288.4 2.3 reshape.132
  293.4 18.0 %copy.33 = bf16[2,2,1601,256]{3,1,2,0:T(2,128)(2,1)S(1)} copy(bf16[2,2,1601,256]{3,2,0,1:T(8,128)(2,1)S(1)} %maximum_bitcast_fusion) | data formatting | bytes 6557696 | tf_op jit(solution)/shard_map/transpose | solution.py:87
  311.5 6.0 %collective-permute-done = bf16[2,2,1601,256]{3,1,2,0:T(2,128)(2,1)} collective-permute-done((bf16[2,2,1601,256]{3,1,2,0:T(2,128)(2,1)S(1)}, bf16[2,2,1601,256]{3,1,2,0:T(2,128)(2,1)}, u32[]{:S(2)}, u32[]{:S(2)}) %collective-permute-start) | collective-permute-done | bytes 3278880 | tf_op jit(solution)/shard_map/ppermute | solution.py:16
  317.4 3.6 broadcast_select_fusion.3
  321.1 3.7 pad_maximum_fusion
  324.8 26.9 %copy.36 = bf16[4,2,1601,256]{3,0,2,1:T(4,128)(2,1)} copy(bf16[4,2,1601,256]{3,2,0,1:T(8,128)(2,1)} %pad_maximum_fusion) | data formatting | bytes 13115392 | tf_op jit(solution)/shard_map/concatenate | solution.py:39
  351.8 1.5 collective-permute-start.1
  353.3 1.4 fusion.23
  361.5 1.2 fusion.17
  362.8 132.6 %collective-permute-done.1 = bf16[4,2,1601,256]{3,0,2,1:T(4,128)(2,1)} collective-permute-done((bf16[4,2,1601,256]{3,0,2,1:T(4,128)(2,1)}, bf16[4,2,1601,256]{3,0,2,1:T(4,128)(2,1)}, u32[]{:S(2)}, u32[]{:S(2)}) %collective-permute-start.1) | collective-permute-done | bytes 6557728 | tf_op jit(solution)/shard_map/ppermute | solution.py:16
  495.4 6.0 %broadcast_select_fusion.1 = (bf16[4,2,1601,256]{3,2,0,1:T(8,128)(2,1)S(1)}, bf16[4,2,1601,256]{3,2,0,1:T(8,128)(2,1)S(1)}) fusion(pred[]{:T(512)S(6)} %eq.49, bf16[4,2,1601,256]{3,0,2,1:T(4,128)(2,1)} %collective-permute-done.1, bf16[2,2,1601,256]{3,2,0,1:T(8,128)(2,1)} %copy-done, bf16[2,2,1601,256]{3,2,0,1:T(8,128)(2,1)S(1)} %get-tuple-element.11), kind=kLoop, calls=%fused_computation.20 | loop fusion | flops 9836544 | bytes 26230784 | tf_op jit(solution)/shard_map/jit(_where)/select_n | solution.py:40
  501.3 2.8 fusion.11
  504.1 1.7 convert_reduce_fusion.2
  505.9 1.0 fusion.16
  506.9 1.8 convert_reduce_fusion
  508.7 1.7 convert_reduce_fusion.1
  510.4 1.8 convert_reduce_fusion.3
  512.2 1.0 convolution_add_fusion.2
  513.2 1.0 convolution_add_fusion.1
  514.3 1.0 fusion.15
  (32 shorter events, 6.9 us)
Async XLA Ops:
  6.5 281.8 %reduce-scatter.2.cloned.1.call-start = ((), (), s32[]{:S(2)}) async-start(), calls=%async_computation.1 | async-start | bytes 16424960 | tf_op jit(solution)/shard_map/reduce_scatter | solution.py:61
  290.6 1.3 copy-start.5
  291.9 1.5 copy-start.1
  293.0 18.4 %copy-start.2 = (bf16[2,2,1601,128]{3,2,1,0:T(8,128)(2,1)}, bf16[2,2,1601,128]{3,2,1,0:T(8,128)(2,1)S(1)}, u32[]{:S(2)}) copy-start(bf16[2,2,1601,128]{3,2,1,0:T(8,128)(2,1)S(1)} %fusion.3) | copy-start | bytes 4918276
  311.4 6.0 %collective-permute-start = (bf16[2,2,1601,256]{3,1,2,0:T(2,128)(2,1)S(1)}, bf16[2,2,1601,256]{3,1,2,0:T(2,128)(2,1)}, u32[]{:S(2)}, u32[]{:S(2)}) collective-permute-start(bf16[2,2,1601,256]{3,1,2,0:T(2,128)(2,1)S(1)} %copy.33), channel_id=1, source_target_pairs={{0,4},{4,0},{8,12},{12,8},{16,20},{20,16},{24,28},{28,24},{1,5},{5... | collective-permute-start | bytes 9836552 | tf_op jit(solution)/shard_map/ppermute | solution.py:16
  321.1 3.8 copy-start
  324.8 33.6 %copy-start.4 = (bf16[1,64,2048]{2,1,0:T(8,128)(2,1)S(1)}, bf16[1,64,2048]{2,1,0:T(8,128)(2,1)}, u32[]{:S(2)}) copy-start(bf16[1,64,2048]{2,1,0:T(8,128)(2,1)} %param.11) | copy-start | bytes 786436
  351.8 143.6 %collective-permute-start.1 = (bf16[4,2,1601,256]{3,0,2,1:T(4,128)(2,1)}, bf16[4,2,1601,256]{3,0,2,1:T(4,128)(2,1)}, u32[]{:S(2)}, u32[]{:S(2)}) collective-permute-start(bf16[4,2,1601,256]{3,0,2,1:T(4,128)(2,1)} %copy.36), channel_id=1, source_target_pairs={{0,8},{4,12},{8,0},{12,4},{16,24},{20,28},{24,16},{28,20},{1,9},{5... | collective-permute-start | bytes 19673096 | tf_op jit(solution)/shard_map/ppermute | solution.py:16
  358.6 0.8 copy-start.3
Sparse Core Ops, SparseCore 0:
  64.4 223.8 reduce-scatter.1
where the time goes:
time: 524 us; the launch traced here: 523 us
  waiting for transfers between devices  363 us (69%)
  local copies, waits for them, and re-layouts  74.3 us (14%)
  matrix products  45.7 us (9%)
  other arithmetic  21.6 us (4%)
  between operations  17.5 us (3%)
    reduce_scatter x1, waiting for transfers between devices, local(): lax.psum_scatter(jnp.einsum('rw,wkc->krc', flat_rows, projection, preferr...  224 us
    ppermute x2, waiting for transfers between devices, swapped(): lax.ppermute(array, axis, [(i, i ^ 1 << distance) for i in range(lax.axis...  139 us
    dot_general x1, matrix products, local(): jnp.einsum('rw,wkc->krc', flat_rows, projection, preferred_element_type=j...  34.6 us
    concatenate x1, local copies, waits for them, and re-layouts, order_pair(): jnp.concatenate([jnp.where(upper_half, peer_part, own_part), jnp.where(up...  26.9 us
    transpose x1, local copies, waits for them, and re-layouts, local(): shared = prepared.transpose(1, 0, 2, 3)  18 us
    unnamed x14, local copies, waits for them, and re-layouts  12.9 us
    reshape x1, local copies, waits for them, and re-layouts, local(): flat_rows = tile_features.reshape(slots_here * tile_rows, width_here)  11.3 us
  transfers between devices with their start and end apart: 3, of which 3 were waited for; matrix products, arithmetic and copies ran while one was open for 1% of the time, Pallas kernels for 0%

commit v1 on v0

v1 whole, which is shorter than its diff:
```python
import math

import jax
import jax.numpy as jnp
from jax import lax
from jax.experimental import pallas as pl
from jax.experimental.pallas import tpu as pltpu
from jax.sharding import PartitionSpec as P

HEADS = 64
KVH = 8
HD = 128
MAXT = 4
GROUP = 4
NZ = 4
SLOTS_HERE = 2
ROWS = 320
UNIT = 5
LANES = 512
SKEW = 2
KHALF = KVH // 2
PER_K = SLOTS_HERE * UNIT
STEPS = KHALF * PER_K
LAST = (NZ - 1) * SKEW
MESH = pl.DeviceIdType.MESH
F32 = jnp.float32
BF16 = jnp.bfloat16


def weight_head(direction, kk):
    return KHALF + kk if direction == 0 else (kk + 2) % KHALF


def kernel(
    feat, tail, weight, query, qgain, kgain, meta, out,
    fbuf, wbuf, acc, tacc, qall, mall, qcur, num, den, csum, dsum, sbuf, rbuf, obuf, nbuf,
    fsem, wsem, csend, crecv, tsend, trecv, qzs, qzr, qfs, qfr, ms, mr, ss, sr, os_, or_,
):
    dp = lax.axis_index("dp")
    z = lax.axis_index("head")
    g = lax.rem(dp, GROUP)
    base = dp - g
    is_end = (z == 0) | (z == NZ - 1)
    peers = [lax.rem(g + o, GROUP) for o in range(1, GROUP)]
    sources = [lax.rem(g + GROUP - o, GROUP) for o in range(1, GROUP)]
    beside = jnp.where(z == 0, 1, jnp.where(z == 1, 0, jnp.where(z == 2, 3, 2)))
    final = jnp.where(z == 0, 1, 0)

    def weight_copy(direction, kk):
        return pltpu.make_async_copy(
            weight.at[weight_head(direction, kk)], wbuf.at[direction, kk], wsem.at[direction, kk]
        )

    def feat_copy(i):
        s, c = i // UNIT, lax.rem(i, UNIT)
        rows = pl.ds(pl.multiple_of(c * ROWS, ROWS), ROWS)
        return pltpu.make_async_copy(feat.at[s, rows], fbuf.at[s, c], fsem.at[i])

    for direction in range(2):
        weight_copy(direction, 0).start()
    for i in range(PER_K):
        feat_copy(i).start()
    for kk in range(1, KHALF):
        for direction in range(2):
            weight_copy(direction, kk).start()

    barrier = pltpu.get_barrier_semaphore()
    for p in peers:
        pl.semaphore_signal(barrier, inc=1, device_id={"dp": base + p}, device_id_type=MESH)

    @pl.when(z > 0)
    def _():
        pl.semaphore_signal(barrier, inc=1, device_id={"head": z - 1}, device_id_type=MESH)

    @pl.when(z < NZ - 1)
    def _():
        pl.semaphore_signal(barrier, inc=1, device_id={"head": z + 1}, device_id_type=MESH)

    for h in range(2 * KVH):
        block = query[0, :, h * HD:(h + 1) * HD].astype(F32)
        squares = jnp.mean(block * block, axis=-1, keepdims=True)
        normed = block * lax.rsqrt(squares + 1e-05) * qgain[...]
        qall[g, 2 + h // 8, (h % 8) * 64:(h % 8 + 1) * 64, :] = normed.astype(BF16)
    mall[g] = meta[...]

    @pl.when(is_end)
    def _():
        pl.semaphore_wait(barrier, GROUP)

    @pl.when(jnp.logical_not(is_end))
    def _():
        pl.semaphore_wait(barrier, GROUP + 1)

    def q_up(dst_half, row):
        return pltpu.make_async_remote_copy(
            src_ref=qall.at[row, pl.ds(2, 2)], dst_ref=qall.at[row, pl.ds(dst_half, 2)],
            send_sem=qzs, recv_sem=qzr, device_id={"head": beside}, device_id_type=MESH,
        )

    def q_forward(half, o, row):
        return pltpu.make_async_remote_copy(
            src_ref=qall.at[row, pl.ds(2 * half, 2)], dst_ref=qall.at[row, pl.ds(2 * half, 2)],
            send_sem=qfs.at[half, o], recv_sem=qfr.at[half, o],
            device_id={"dp": base + peers[o]}, device_id_type=MESH,
        )

    def meta_forward(o, row):
        return pltpu.make_async_remote_copy(
            src_ref=mall.at[row], dst_ref=mall.at[row], send_sem=ms.at[o], recv_sem=mr.at[o],
            device_id={"dp": base + peers[o]}, device_id_type=MESH,
        )

    def part_send(kk, o, src_row, dst_row):
        return pltpu.make_async_remote_copy(
            src_ref=sbuf.at[kk, src_row], dst_ref=rbuf.at[kk, dst_row],
            send_sem=ss.at[kk, o], recv_sem=sr.at[kk, o],
            device_id={"dp": base + peers[o]}, device_id_type=MESH,
        )

    def out_send():
        return pltpu.make_async_remote_copy(
            src_ref=obuf.at[pl.ds(0, 2)], dst_ref=nbuf, send_sem=os_, recv_sem=or_,
            device_id={"head": beside}, device_id_type=MESH,
        )

    @pl.when(jnp.logical_not(is_end))
    def _():
        q_up(0, g).start()

    @pl.when(is_end)
    def _():
        for o in range(GROUP - 1):
            meta_forward(o, g).start()
            q_forward(1, o, g).start()

    def chain(direction, i):
        step = 1 if direction == 0 else -1
        return pltpu.make_async_remote_copy(
            src_ref=acc.at[direction, i], dst_ref=acc.at[direction, i],
            send_sem=csend.at[direction, i], recv_sem=crecv.at[direction, i],
            device_id={"head": z + step}, device_id_type=MESH,
        )

    def tail_chain(direction, kk):
        step = 1 if direction == 0 else -1
        return pltpu.make_async_remote_copy(
            src_ref=tacc.at[direction, kk], dst_ref=tacc.at[direction, kk],
            send_sem=tsend.at[direction, kk], recv_sem=trecv.at[direction, kk],
            device_id={"head": z + step}, device_id_type=MESH,
        )

    def add_link(direction, i):
        first = (z == 0) if direction == 0 else (z == NZ - 1)
        last = (z == NZ - 1) if direction == 0 else (z == 0)
        kk = i // PER_K
        s = lax.rem(i, PER_K) // UNIT
        c = lax.rem(i, UNIT)

        @pl.when(lax.rem(i, PER_K) == 0)
        def _():
            part = jnp.dot(tail[...], wbuf[direction, kk], preferred_element_type=F32)

            @pl.when(first)
            def _():
                tacc[direction, kk] = part.astype(BF16)

            @pl.when(jnp.logical_not(first))
            def _():
                tail_chain(direction, kk).wait_recv()
                tacc[direction, kk] = (tacc[direction, kk].astype(F32) + part).astype(BF16)

            @pl.when(jnp.logical_not(last))
            def _():
                tail_chain(direction, kk).start()

        part = jnp.dot(fbuf[s, c], wbuf[direction, kk], preferred_element_type=F32)

        @pl.when(first)
        def _():
            acc[direction, i] = part.astype(BF16)

        @pl.when(jnp.logical_not(first))
        def _():
            chain(direction, i).wait_recv()
            acc[direction, i] = (acc[direction, i].astype(F32) + part).astype(BF16)

        @pl.when(jnp.logical_not(last))
        def _():
            chain(direction, i).start()

    def weigh(kv, valid):
        keys = kv[:, :HD].astype(F32)
        squares = jnp.mean(keys * keys, axis=-1, keepdims=True)
        normed = (keys * lax.rsqrt(squares + 1e-05) * kgain[...]).astype(BF16)
        scores = lax.dot_general(
            normed, qcur[...], (((1,), (1,)), ((), ())), preferred_element_type=F32
        ) * (1.0 / math.sqrt(HD))
        weights = jnp.exp(scores)
        if valid is not None:
            weights = jnp.where(valid, weights, 0.0)
        weights = weights.astype(BF16)
        denominator = jnp.sum(weights.astype(F32), axis=0, keepdims=True)
        numerator = lax.dot_general(
            kv[:, HD:], weights, (((0,), (0,)), ((), ())), preferred_element_type=F32
        )
        return numerator, denominator

    def hits(j, s):
        rows = mall[j]
        hit = jnp.where(rows[MAXT:2 * MAXT] == dp * SLOTS_HERE + s, 1, 0)
        match = jnp.max(hit, axis=0, keepdims=True)
        usable = jnp.max(hit * rows[:MAXT], axis=0, keepdims=True)
        return match, usable

    def attend(d):
        kk = d // PER_K
        s = lax.rem(d, PER_K) // UNIT

        @pl.when(lax.rem(d, UNIT) == 0)
        def _():
            chosen = jnp.zeros((LANES, HD), F32)
            for j in range(GROUP):
                match, _u = hits(j, s)
                chosen = chosen + match[:, :HD].astype(F32) * qall[j, kk].astype(F32)
            qcur[...] = chosen.astype(BF16)
            row = lax.broadcasted_iota(jnp.int32, (16, LANES), 0)
            n0, d0 = weigh(tacc[final, kk], row == s)
            num[...] = n0
            den[...] = d0

        n1, d1 = weigh(acc[final, d], None)
        num[...] += n1
        den[...] += d1

        @pl.when(lax.rem(d, PER_K) == UNIT - 1)
        def _():
            for j in range(GROUP):
                _m, usable = hits(j, s)
                csum[j] = jnp.where(usable == 1, num[...], 0.0)
                dsum[j] = jnp.where(usable == 1, den[...], 0.0)

        @pl.when(lax.rem(d, PER_K) == PER_K - 1)
        def _():
            for j in range(GROUP):
                _m, usable = hits(j, s)
                total = csum[j] + jnp.where(usable == 1, num[...], 0.0)
                below = dsum[j] + jnp.where(usable == 1, den[...], 0.0)
                high = below.astype(BF16).astype(F32)
                row = lax.broadcasted_iota(jnp.int32, (16, LANES), 0)
                pair = jnp.where(row == 0, high, jnp.where(row == 1, below - high, 0.0))
                sbuf[kk, j, :HD, :] = total.astype(BF16)
                sbuf[kk, j, HD:, :] = pair.astype(BF16)
            for o in range(GROUP - 1):
                part_send(kk, o, peers[o], g).start()

    def finish(kk):
        for o in range(GROUP - 1):
            part_send(kk, o, sources[o], sources[o]).wait_recv()
        total = sbuf[kk, g].astype(F32)
        for o in range(GROUP - 1):
            total = total + rbuf[kk, sources[o]].astype(F32)
        below = total[HD:HD + 1] + total[HD + 1:HD + 2]
        live = jnp.max(mall[g][:MAXT], axis=0, keepdims=True) == 1
        inverse = 1.0 / jnp.where(live, below, 1.0)
        result = jnp.where(live, total[:HD] * inverse, 0.0)
        obuf[kk] = result.T.astype(BF16)

        @pl.when(kk == 1)
        def _():
            out_send().start()

    def body(t, carry):
        @pl.when(t < PER_K)
        def _():
            feat_copy(t).wait()

        for kk in range(KHALF):
            @pl.when(t == kk * PER_K)
            def _():
                for direction in range(2):
                    weight_copy(direction, kk).wait()

        up = t - SKEW * z
        down = t - SKEW * (NZ - 1 - z)
        d = t - LAST

        @pl.when((up >= 0) & (up < STEPS))
        def _():
            add_link(0, up)

        @pl.when((down >= 0) & (down < STEPS))
        def _():
            add_link(1, down)

        @pl.when(is_end & (t == 1))
        def _():
            q_up(0, g).wait_recv()
            for o in range(GROUP - 1):
                q_forward(0, o, g).start()

        @pl.when(is_end & (d == 0))
        def _():
            for o in range(GROUP - 1):
                meta_forward(o, sources[o]).wait_recv()
                for half in range(2):
                    q_forward(half, o, sources[o]).wait_recv()

        @pl.when(is_end & (d >= 0) & (d < STEPS))
        def _():
            attend(d)

        late = d - PER_K - UNIT + 1

        @pl.when(is_end & (late >= 0) & (lax.rem(late + PER_K, PER_K) == 0))
        def _():
            finish(late // PER_K)

        return carry

    lax.fori_loop(0, STEPS + LAST + UNIT, body, 0)

    @pl.when(is_end)
    def _():
        for h in range(2 * KVH):
            out[0, :, h * HD:(h + 1) * HD] = obuf[2 + h // 8, (h % 8) * 64:(h % 8 + 1) * 64, :]
        out_send().wait_send()
        for o in range(GROUP - 1):
            meta_forward(o, g).wait_send()
            for half in range(2):
                q_forward(half, o, g).wait_send()
            for kk in range(KHALF):
                part_send(kk, o, peers[o], g).wait_send()

    @pl.when(jnp.logical_not(is_end))
    def _():
        out_send().wait_recv()
        for h in range(2 * KVH):
            out[0, :, h * HD:(h + 1) * HD] = nbuf[h // 8, (h % 8) * 64:(h % 8 + 1) * 64, :]
        q_up(0, g).wait_send()

    def drain(direction):
        def each(i, carry):
            chain(direction, i).wait_send()
            return carry

        lax.fori_loop(0, STEPS, each, 0)
        for kk in range(KHALF):
            tail_chain(direction, kk).wait_send()

    @pl.when(z < NZ - 1)
    def _():
        drain(0)

    @pl.when(z > 0)
    def _():
        drain(1)


def local(
    tile_features, projection, queries, query_gain, key_gain,
    tile_count, tile_slot, cross_mask, prompt_length,
):
    width = tile_features.shape[2]
    prompt_rows = queries.shape[1]
    whole_rows = UNIT * ROWS
    tail = jnp.pad(tile_features[:, whole_rows, :], ((0, 16 - SLOTS_HERE), (0, 0)))
    weight = projection.transpose(1, 0, 2)
    tiles = jnp.arange(MAXT, dtype=jnp.int32)
    rows = jnp.arange(prompt_rows, dtype=jnp.int32)
    usable = (
        (cross_mask[0].T == 1)
        & (tiles[:, None] < tile_count[0])
        & (rows[None, :] < prompt_length[0])
    ).astype(jnp.int32)
    usable = jnp.tile(usable, (1, HEADS // KVH))
    held = jnp.where(tiles < tile_count[0], tile_slot[0], -1)
    meta = jnp.concatenate([usable, jnp.broadcast_to(held[:, None], (MAXT, LANES))], axis=0)

    vmem = pl.BlockSpec(memory_space=pltpu.VMEM)
    hbm = pl.BlockSpec(memory_space=pl.ANY)
    dma = pltpu.SemaphoreType.DMA
    return pl.pallas_call(
        kernel,
        out_shape=jax.ShapeDtypeStruct(queries.shape, BF16),
        in_specs=[hbm, vmem, hbm, vmem, vmem, vmem, vmem],
        out_specs=vmem,
        scratch_shapes=[
            pltpu.VMEM((SLOTS_HERE, UNIT, ROWS, width), BF16),
            pltpu.VMEM((2, KHALF, width, 2 * HD), BF16),
            pltpu.VMEM((2, STEPS, ROWS, 2 * HD), BF16),
            pltpu.VMEM((2, KHALF, 16, 2 * HD), BF16),
            pltpu.VMEM((GROUP, KHALF, LANES, HD), BF16),
            pltpu.VMEM((GROUP, 2 * MAXT, LANES), jnp.int32),
            pltpu.VMEM((LANES, HD), BF16),
            pltpu.VMEM((HD, LANES), F32),
            pltpu.VMEM((1, LANES), F32),
            pltpu.VMEM((GROUP, HD, LANES), F32),
            pltpu.VMEM((GROUP, 1, LANES), F32),
            pltpu.VMEM((KHALF, GROUP, HD + 16, LANES), BF16),
            pltpu.VMEM((KHALF, GROUP, HD + 16, LANES), BF16),
            pltpu.VMEM((KHALF, LANES, HD), BF16),
            pltpu.VMEM((2, LANES, HD), BF16),
            dma((PER_K,)),
            dma((2, KHALF)),
            dma((2, STEPS)),
            dma((2, STEPS)),
            dma((2, KHALF)),
            dma((2, KHALF)),
            dma,
            dma,
            dma((2, GROUP - 1)),
            dma((2, GROUP - 1)),
            dma((GROUP - 1,)),
            dma((GROUP - 1,)),
            dma((KHALF, GROUP - 1)),
            dma((KHALF, GROUP - 1)),
            dma,
            dma,
        ],
        compiler_params=pltpu.CompilerParams(
            collective_id=0, has_side_effects=True, vmem_limit_bytes=58 * 1024 * 1024
        ),
        cost_estimate=pl.CostEstimate(
            flops=30_000_000_000, bytes_accessed=25_000_000, transcendentals=7_000_000
        ),
    )(
        tile_features, tail, weight, queries,
        query_gain.reshape(1, HD), key_gain.reshape(1, HD), meta,
    )


def solution(mesh):
    in_specs = (
        P("dp", None, "head"),
        P("head", None, None),
        P("dp", None, "head"),
        P(),
        P(),
        P("dp"),
        P("dp", None),
        P("dp", None, None),
        P("dp"),
    )
    out_specs = P("dp", None, "head")
    return jax.shard_map(local, mesh=mesh, in_specs=in_specs, out_specs=out_specs, check_vma=False)
```

time: 524 us -> 206 us (0.39)
  waiting for transfers between devices: 363 us -> 0 us
  Pallas kernels: 0 us -> 178 us
  local copies, waits for them, and re-layouts: 74.3 us -> 23 us
  matrix products: 45.7 us -> 0 us
  other arithmetic: 21.6 us -> 2.09 us
  between operations: 17.5 us -> 1.32 us
    reduce_scatter x1 -> x0, waiting for transfers between devices: 224 us -> none  [local(): lax.psum_scatter(jnp.einsum('rw,wkc->krc', flat_rows, projection, preferr...]
    pallas_call x0 -> x1, Pallas kernels: none -> 178 us  [local(): pl.pallas_call(kernel, out_shape=jax.ShapeDtypeStruct(queries.shape, BF16...]
    ppermute x2 -> x0, waiting for transfers between devices: 139 us -> none  [swapped(): lax.ppermute(array, axis, [(i, i ^ 1 << distance) for i in range(lax.axis...]
    dot_general x9 -> x0, matrix products: 45.7 us -> none  [the longest x1 34.6 us: local(): jnp.einsum('rw,wkc->krc', flat_rows, projection, preferred_element_type=j...]
    concatenate x1, local copies, waits for them, and re-layouts: 26.9 us -> 0.08 us  [local(): jnp.concatenate([usable, jnp.broadcast_to(held[:, None], (MAXT, LANES))],...]
    transpose x1 -> x0, local copies, waits for them, and re-layouts: 18 us -> none  [local(): shared = prepared.transpose(1, 0, 2, 3)]
    reshape x2 -> x0, local copies, waits for them, and re-layouts: 13.5 us -> none  [the longest x1 11.3 us: local(): flat_rows = tile_features.reshape(slots_here * tile_rows, width_here)]
    select_n x3 -> x1, other arithmetic: 9.63 us -> 0.66 us  [local(): held = jnp.where(tiles < tile_count[0], tile_slot[0], -1)]
  transfers between devices with their start and end apart: 3 -> 0, of which waited for: 3 -> 0; matrix products, arithmetic and copies ran while one was open for 1% -> 0% of each run, Pallas kernels for 0% -> 0%
where the time goes in v1:
time: 206 us; the launch traced here: 205 us
  Pallas kernels  178 us (86%)
  local copies, waits for them, and re-layouts  23 us (11%)
  other arithmetic  2.09 us (1%)
    pallas_call x1, Pallas kernels, local(): pl.pallas_call(kernel, out_shape=jax.ShapeDtypeStruct(queries.shape, BF16...  178 us
    unnamed x3, local copies, waits for them, and re-layouts  21.5 us

profile of v1, /device:TPU:0, one launch (start us, length us, event | category | flops | bytes accessed | tf_op | source)
XLA Modules:
  0.0 204.6 jit_solution(14716848433712768482)
XLA Ops:
  1.3 0.7 bitcast_select_fusion
  2.0 0.1 pad.6.clone
  2.1 0.8 convert_bitcast_fusion
  2.8 0.7 slice_bitcast_fusion
  3.5 0.1 tile.10
  3.6 0.7 pad_add_fusion.meta
  4.3 0.6 pad.4.tail
  4.9 7.9 %copy.13 = bf16[1920,8,256]{2,0,1:T(8,128)(2,1)} copy(bf16[1920,8,256]{2,1,0:T(8,128)(2,1)} %param.10) | data formatting | bytes 15728640 | tf_op args[1]
  12.8 11.9 %copy.11.feat = bf16[2,1601,1920]{2,1,0:T(8,128)(2,1)} copy(bf16[2,1601,1920]{2,0,1:T(2,128)(2,1)} %param.9) | data formatting | bytes 24591360 | tf_op args[0]
  24.7 178.2 %shard_map.91 = bf16[1,64,2048]{2,1,0:T(8,128)(2,1)} custom-call(bf16[2,1601,1920]{2,1,0:T(8,128)(2,1)} %copy.11.feat, bf16[16,1920]{1,0:T(8,128)(2,1)} %pad.4.tail, bf16[8,1920,256]{2,1,0:T(8,128)(2,1)} %bitcast.22, bf16[1,64,2048]{2,1,0:T(8,128)(2,1)} %query.1, f32[1,128]{1,0:T(1,128)} %bitcast.23, f32[1,128]{1,0:T(1,128)} %bitcast.24, ...), custom_call_target="tpu_custom_call" | custom-call | flops 30000001024 | bytes 25000000 | tf_op jit(solution)/shard_map/pallas_call | solution.py:382
  202.9 1.7 copy.17
  (3 shorter events, 0.0 us)

commit v2 on v1

--- a/solution.py
+++ b/solution.py
@@ -14,13 +14,14 @@
 GROUP = 4
 NZ = 4
 SLOTS_HERE = 2
-ROWS = 320
-UNIT = 5
+ROWS = 160
+UNIT = 10
 LANES = 512
 SKEW = 2
+LAG = 5
 KHALF = KVH // 2
-PER_K = SLOTS_HERE * UNIT
-STEPS = KHALF * PER_K
+PAIRS = ROWS * SLOTS_HERE
+STEPS = KHALF * UNIT
 LAST = (NZ - 1) * SKEW
 MESH = pl.DeviceIdType.MESH
 F32 = jnp.float32
@@ -32,9 +33,9 @@
 
 
 def kernel(
-    feat, tail, weight, query, qgain, kgain, meta, out,
-    fbuf, wbuf, acc, tacc, qall, mall, qcur, num, den, csum, dsum, sbuf, rbuf, obuf, nbuf,
-    fsem, wsem, csend, crecv, tsend, trecv, qzs, qzr, qfs, qfr, ms, mr, ss, sr, os_, or_,
+    feat, weight, query, qgain, kgain, meta, out,
+    fraw, traw, fbuf, tail, kvf, wbuf, acc, tacc, qall, mall, qcur, num, den, sbuf, rbuf, obuf, nbuf,
+    fsem, xsem, wsem, csend, crecv, tsend, trecv, qzs, qzr, qfs, qfr, ms, mr, ss, sr, os_, or_,
 ):
     dp = lax.axis_index("dp")
     z = lax.axis_index("head")
@@ -52,13 +53,20 @@
         )
 
     def feat_copy(i):
-        s, c = i // UNIT, lax.rem(i, UNIT)
-        rows = pl.ds(pl.multiple_of(c * ROWS, ROWS), ROWS)
-        return pltpu.make_async_copy(feat.at[s, rows], fbuf.at[s, c], fsem.at[i])
+        return pltpu.make_async_copy(
+            feat.at[pl.ds(i * ROWS, ROWS)], fraw.at[i], fsem.at[i]
+        )
+
+    def tail_copy():
+        return pltpu.make_async_copy(
+            feat.at[pl.ds(UNIT * ROWS, 1)], traw.at[pl.ds(0, 1)], xsem
+        )
 
     for direction in range(2):
         weight_copy(direction, 0).start()
-    for i in range(PER_K):
+    traw[...] = jnp.zeros_like(traw)
+    tail_copy().start()
+    for i in range(UNIT):
         feat_copy(i).start()
     for kk in range(1, KHALF):
         for direction in range(2):
@@ -152,11 +160,10 @@
     def add_link(direction, i):
         first = (z == 0) if direction == 0 else (z == NZ - 1)
         last = (z == NZ - 1) if direction == 0 else (z == 0)
-        kk = i // PER_K
-        s = lax.rem(i, PER_K) // UNIT
+        kk = i // UNIT
         c = lax.rem(i, UNIT)
 
-        @pl.when(lax.rem(i, PER_K) == 0)
+        @pl.when(lax.rem(i, UNIT) == 0)
         def _():
             part = jnp.dot(tail[...], wbuf[direction, kk], preferred_element_type=F32)
 
@@ -173,7 +180,7 @@
             def _():
                 tail_chain(direction, kk).start()
 
-        part = jnp.dot(fbuf[s, c], wbuf[direction, kk], preferred_element_type=F32)
+        part = jnp.dot(fbuf[c], wbuf[direction, kk], preferred_element_type=F32)
 
         @pl.when(first)
         def _():
@@ -188,12 +195,12 @@
         def _():
             chain(direction, i).start()
 
-    def weigh(kv, valid):
-        keys = kv[:, :HD].astype(F32)
+    def weigh(kv, s, valid):
+        keys = kv[:, :HD]
         squares = jnp.mean(keys * keys, axis=-1, keepdims=True)
         normed = (keys * lax.rsqrt(squares + 1e-05) * kgain[...]).astype(BF16)
         scores = lax.dot_general(
-            normed, qcur[...], (((1,), (1,)), ((), ())), preferred_element_type=F32
+            normed, qcur[s], (((1,), (1,)), ((), ())), preferred_element_type=F32
         ) * (1.0 / math.sqrt(HD))
         weights = jnp.exp(scores)
         if valid is not None:
@@ -201,7 +208,7 @@
         weights = weights.astype(BF16)
         denominator = jnp.sum(weights.astype(F32), axis=0, keepdims=True)
         numerator = lax.dot_general(
-            kv[:, HD:], weights, (((0,), (0,)), ((), ())), preferred_element_type=F32
+            kv[:, HD:].astype(BF16), weights, (((0,), (0,)), ((), ())), preferred_element_type=F32
         )
         return numerator, denominator
 
@@ -213,40 +220,41 @@
         return match, usable
 
     def attend(d):
-        kk = d // PER_K
-        s = lax.rem(d, PER_K) // UNIT
+        kk = d // UNIT
 
         @pl.when(lax.rem(d, UNIT) == 0)
         def _():
-            chosen = jnp.zeros((LANES, HD), F32)
+            row = lax.broadcasted_iota(jnp.int32, (16, LANES), 0)
+            for s in range(SLOTS_HERE):
+                chosen = jnp.zeros((LANES, HD), F32)
+                for j in range(GROUP):
+                    match, _u = hits(j, s)
+                    chosen = chosen + match[:, :HD].astype(F32) * qall[j, kk].astype(F32)
+                qcur[s] = chosen.astype(BF16)
+                n0, d0 = weigh(tacc[final, kk].astype(F32), s, row == s)
+                num[s] = n0
+                den[s] = d0
+
+        kvf[0] = acc[final, d, :, :HD].astype(F32)
+        kvf[1] = acc[final, d, :, HD:].astype(F32)
+        for s in range(SLOTS_HERE):
+            every = pl.ds(s, ROWS, stride=SLOTS_HERE)
+            own = jnp.concatenate([kvf[0, every, :], kvf[1, every, :]], axis=1)
+            n1, d1 = weigh(own, s, None)
+            num[s] += n1
+            den[s] += d1
+
+        @pl.when(lax.rem(d, UNIT) == UNIT - 1)
+        def _():
+            row = lax.broadcasted_iota(jnp.int32, (16, LANES), 0)
             for j in range(GROUP):
-                match, _u = hits(j, s)
-                chosen = chosen + match[:, :HD].astype(F32) * qall[j, kk].astype(F32)
-            qcur[...] = chosen.astype(BF16)
-            row = lax.broadcasted_iota(jnp.int32, (16, LANES), 0)
-            n0, d0 = weigh(tacc[final, kk], row == s)
-            num[...] = n0
-            den[...] = d0
-
-        n1, d1 = weigh(acc[final, d], None)
-        num[...] += n1
-        den[...] += d1
-
-        @pl.when(lax.rem(d, PER_K) == UNIT - 1)
-        def _():
-            for j in range(GROUP):
-                _m, usable = hits(j, s)
-                csum[j] = jnp.where(usable == 1, num[...], 0.0)
-                dsum[j] = jnp.where(usable == 1, den[...], 0.0)
-
-        @pl.when(lax.rem(d, PER_K) == PER_K - 1)
-        def _():
-            for j in range(GROUP):
-                _m, usable = hits(j, s)
-                total = csum[j] + jnp.where(usable == 1, num[...], 0.0)
-                below = dsum[j] + jnp.where(usable == 1, den[...], 0.0)
+                total = jnp.zeros((HD, LANES), F32)
+                below = jnp.zeros((1, LANES), F32)
+                for s in range(SLOTS_HERE):
+                    _m, usable = hits(j, s)
+                    total = total + jnp.where(usable == 1, num[s], 0.0)
+                    below = below + jnp.where(usable == 1, den[s], 0.0)
                 high = below.astype(BF16).astype(F32)
-                row = lax.broadcasted_iota(jnp.int32, (16, LANES), 0)
                 pair = jnp.where(row == 0, high, jnp.where(row == 1, below - high, 0.0))
                 sbuf[kk, j, :HD, :] = total.astype(BF16)
                 sbuf[kk, j, HD:, :] = pair.astype(BF16)
@@ -270,12 +278,18 @@
             out_send().start()
 
     def body(t, carry):
-        @pl.when(t < PER_K)
+        @pl.when(t < UNIT)
         def _():
             feat_copy(t).wait()
+            fbuf[t] = fraw[t].reshape(PAIRS, fraw.shape[-1])
+
+        @pl.when(t == 0)
+        def _():
+            tail_copy().wait()
+            tail[...] = traw[...].reshape(16, traw.shape[-1])
 
         for kk in range(KHALF):
-            @pl.when(t == kk * PER_K)
+            @pl.when(t == kk * UNIT)
             def _():
                 for direction in range(2):
                     weight_copy(direction, kk).wait()
@@ -309,15 +323,15 @@
         def _():
             attend(d)
 
-        late = d - PER_K - UNIT + 1
-
-        @pl.when(is_end & (late >= 0) & (lax.rem(late + PER_K, PER_K) == 0))
-        def _():
-            finish(late // PER_K)
+        late = d - UNIT - LAG + 1
+
+        @pl.when(is_end & (late >= 0) & (lax.rem(late + UNIT, UNIT) == 0))
+        def _():
+            finish(late // UNIT)
 
         return carry
 
-    lax.fori_loop(0, STEPS + LAST + UNIT, body, 0)
+    lax.fori_loop(0, STEPS + LAST + LAG, body, 0)
 
     @pl.when(is_end)
     def _():
@@ -362,8 +376,6 @@
 ):
     width = tile_features.shape[2]
     prompt_rows = queries.shape[1]
-    whole_rows = UNIT * ROWS
-    tail = jnp.pad(tile_features[:, whole_rows, :], ((0, 16 - SLOTS_HERE), (0, 0)))
     weight = projection.transpose(1, 0, 2)
     tiles = jnp.arange(MAXT, dtype=jnp.int32)
     rows = jnp.arange(prompt_rows, dtype=jnp.int32)
@@ -382,25 +394,28 @@
     return pl.pallas_call(
         kernel,
         out_shape=jax.ShapeDtypeStruct(queries.shape, BF16),
-        in_specs=[hbm, vmem, hbm, vmem, vmem, vmem, vmem],
+        in_specs=[hbm, hbm, vmem, vmem, vmem, vmem],
         out_specs=vmem,
         scratch_shapes=[
-            pltpu.VMEM((SLOTS_HERE, UNIT, ROWS, width), BF16),
+            pltpu.VMEM((UNIT, ROWS, SLOTS_HERE, width), BF16),
+            pltpu.VMEM((8, SLOTS_HERE, width), BF16),
+            pltpu.VMEM((UNIT, PAIRS, width), BF16),
+            pltpu.VMEM((16, width), BF16),
+            pltpu.VMEM((2, PAIRS, HD), F32),
             pltpu.VMEM((2, KHALF, width, 2 * HD), BF16),
-            pltpu.VMEM((2, STEPS, ROWS, 2 * HD), BF16),
+            pltpu.VMEM((2, STEPS, PAIRS, 2 * HD), BF16),
             pltpu.VMEM((2, KHALF, 16, 2 * HD), BF16),
             pltpu.VMEM((GROUP, KHALF, LANES, HD), BF16),
             pltpu.VMEM((GROUP, 2 * MAXT, LANES), jnp.int32),
-            pltpu.VMEM((LANES, HD), BF16),
-            pltpu.VMEM((HD, LANES), F32),
-            pltpu.VMEM((1, LANES), F32),
-            pltpu.VMEM((GROUP, HD, LANES), F32),
-            pltpu.VMEM((GROUP, 1, LANES), F32),
+            pltpu.VMEM((SLOTS_HERE, LANES, HD), BF16),
+            pltpu.VMEM((SLOTS_HERE, HD, LANES), F32),
+            pltpu.VMEM((SLOTS_HERE, 1, LANES), F32),
             pltpu.VMEM((KHALF, GROUP, HD + 16, LANES), BF16),
             pltpu.VMEM((KHALF, GROUP, HD + 16, LANES), BF16),
             pltpu.VMEM((KHALF, LANES, HD), BF16),
             pltpu.VMEM((2, LANES, HD), BF16),
-            dma((PER_K,)),
+            dma((UNIT,)),
+            dma,
             dma((2, KHALF)),
             dma((2, STEPS)),
             dma((2, STEPS)),
@@ -424,7 +439,7 @@
             flops=30_000_000_000, bytes_accessed=25_000_000, transcendentals=7_000_000
         ),
     )(
-        tile_features, tail, weight, queries,
+        tile_features.transpose(1, 0, 2), weight, queries,
         query_gain.reshape(1, HD), key_gain.reshape(1, HD), meta,
     )
 

time: 206 us -> 196 us (0.951)
  local copies, waits for them, and re-layouts: 23 us -> 9.77 us
  Pallas kernels: 178 us -> 181 us
    unnamed x3 -> x2, local copies, waits for them, and re-layouts: 21.5 us -> 9.61 us
    pallas_call x1, Pallas kernels: 178 us -> 181 us  [local(): pl.pallas_call(kernel, out_shape=jax.ShapeDtypeStruct(queries.shape, BF16...]
where the time goes in v2:
time: 196 us; the launch traced here: 194 us
  Pallas kernels  181 us (92%)
  local copies, waits for them, and re-layouts  9.77 us (5%)
  other arithmetic  2.1 us (1%)
    pallas_call x1, Pallas kernels, local(): pl.pallas_call(kernel, out_shape=jax.ShapeDtypeStruct(queries.shape, BF16...  181 us
    unnamed x2, local copies, waits for them, and re-layouts  9.61 us

profile of v2, /device:TPU:0, one launch (start us, length us, event | category | flops | bytes accessed | tf_op | source)
XLA Modules:
  0.0 194.3 jit_solution(15656996214945144458)
XLA Ops:
  1.3 0.7 bitcast_select_fusion
  2.0 0.1 pad.1.clone
  2.1 0.8 convert_bitcast_fusion
  2.8 0.1 tile.10
  2.9 0.7 pad_add_fusion.meta
  3.6 7.9 %copy.12 = bf16[1920,8,256]{2,0,1:T(8,128)(2,1)} copy(bf16[1920,8,256]{2,1,0:T(8,128)(2,1)} %param.10) | data formatting | bytes 15728640 | tf_op args[1]
  11.5 181.1 %shard_map.91 = bf16[1,64,2048]{2,1,0:T(8,128)(2,1)} custom-call(bf16[1601,2,1920]{2,1,0:T(2,128)(2,1)} %bitcast.22, bf16[8,1920,256]{2,1,0:T(8,128)(2,1)} %bitcast.21, bf16[1,64,2048]{2,1,0:T(8,128)(2,1)} %query.1, f32[1,128]{1,0:T(1,128)} %bitcast.23, f32[1,128]{1,0:T(1,128)} %bitcast.24, s32[8,512]{1,0:T(8,128)} %pad_add_fusion.meta), custom_call_target="tpu_custom_call" | custom-call | flops 30000001024 | bytes 25000000 | tf_op jit(solution)/shard_map/pallas_call | solution.py:394
  192.7 1.7 copy.16
  (3 shorter events, 0.0 us)

commit v3 on v2

--- a/solution.py
+++ b/solution.py
@@ -17,23 +17,25 @@
 ROWS = 160
 UNIT = 10
 LANES = 512
-SKEW = 2
+AHEAD = 3
+HALVES = 2
 LAG = 5
 KHALF = KVH // 2
 PAIRS = ROWS * SLOTS_HERE
+PIECE = PAIRS // HALVES
 STEPS = KHALF * UNIT
-LAST = (NZ - 1) * SKEW
+LAST = NZ - 1 + AHEAD
 MESH = pl.DeviceIdType.MESH
 F32 = jnp.float32
 BF16 = jnp.bfloat16
 
 
 def weight_head(direction, kk):
-    return KHALF + kk if direction == 0 else (kk + 2) % KHALF
+    return jnp.where(direction == 0, KHALF + kk, (kk + 2) % KHALF)
 
 
 def kernel(
-    feat, weight, query, qgain, kgain, meta, out,
+    count, slots, length, feat, weight, query, qgain, kgain, mask, out,
     fraw, traw, fbuf, tail, kvf, wbuf, acc, tacc, qall, mall, qcur, num, den, sbuf, rbuf, obuf, nbuf,
     fsem, xsem, wsem, csend, crecv, tsend, trecv, qzs, qzr, qfs, qfr, ms, mr, ss, sr, os_, or_,
 ):
@@ -62,95 +64,109 @@
             feat.at[pl.ds(UNIT * ROWS, 1)], traw.at[pl.ds(0, 1)], xsem
         )
 
-    for direction in range(2):
-        weight_copy(direction, 0).start()
+    near = jnp.where(z < NZ // 2, 0, 1)
+    weight_copy(near, 0).start()
     traw[...] = jnp.zeros_like(traw)
     tail_copy().start()
-    for i in range(UNIT):
+    feat_copy(0).start()
+    weight_copy(1 - near, 0).start()
+
+    barrier = pltpu.get_barrier_semaphore()
+    for p in peers:
+        pl.semaphore_signal(barrier, inc=1, device_id={"dp": base + p}, device_id_type=MESH)
+
+    @pl.when(z > 0)
+    def _():
+        pl.semaphore_signal(barrier, inc=1, device_id={"head": z - 1}, device_id_type=MESH)
+
+    @pl.when(z < NZ - 1)
+    def _():
+        pl.semaphore_signal(barrier, inc=1, device_id={"head": z + 1}, device_id_type=MESH)
+
+    tile = lax.broadcasted_iota(jnp.int32, (MAXT, LANES), 0)
+    prompt = lax.rem(lax.broadcasted_iota(jnp.int32, (MAXT, LANES), 1), 64)
+    seen = jnp.concatenate([mask[0]] * (LANES // 64), axis=1)
+    used = (seen == 1) & (tile < count[0]) & (prompt < length[0])
+    held = jnp.full((MAXT, LANES), -1, jnp.int32)
+    for i in range(MAXT):
+        held = jnp.where((tile == i) & (tile < count[0]), slots[0, i], held)
+    mall[g, :MAXT] = jnp.where(used, 1, 0)
+    mall[g, MAXT:] = held
+
+    @pl.when(is_end)
+    def _():
+        pl.semaphore_wait(barrier, GROUP)
+
+    @pl.when(jnp.logical_not(is_end))
+    def _():
+        pl.semaphore_wait(barrier, GROUP + 1)
+
+    def q_up(dst_half, row):
+        return pltpu.make_async_remote_copy(
+            src_ref=qall.at[row, pl.ds(2, 2)], dst_ref=qall.at[row, pl.ds(dst_half, 2)],
+            send_sem=qzs, recv_sem=qzr, device_id={"head": beside}, device_id_type=MESH,
+        )
+
+    def q_forward(half, o, row):
+        return pltpu.make_async_remote_copy(
+            src_ref=qall.at[row, pl.ds(2 * half, 2)], dst_ref=qall.at[row, pl.ds(2 * half, 2)],
+            send_sem=qfs.at[half, o], recv_sem=qfr.at[half, o],
+            device_id={"dp": base + peers[o]}, device_id_type=MESH,
+        )
+
+    def meta_forward(o, row):
+        return pltpu.make_async_remote_copy(
+            src_ref=mall.at[row], dst_ref=mall.at[row], send_sem=ms.at[o], recv_sem=mr.at[o],
+            device_id={"dp": base + peers[o]}, device_id_type=MESH,
+        )
+
+    def part_send(kk, o, src_row, dst_row):
+        return pltpu.make_async_remote_copy(
+            src_ref=sbuf.at[kk, src_row], dst_ref=rbuf.at[kk, dst_row],
+            send_sem=ss.at[kk, o], recv_sem=sr.at[kk, o],
+            device_id={"dp": base + peers[o]}, device_id_type=MESH,
+        )
+
+    def out_send():
+        return pltpu.make_async_remote_copy(
+            src_ref=obuf.at[pl.ds(0, 2)], dst_ref=nbuf, send_sem=os_, recv_sem=or_,
+            device_id={"head": beside}, device_id_type=MESH,
+        )
+
+    for i in range(1, UNIT):
         feat_copy(i).start()
     for kk in range(1, KHALF):
         for direction in range(2):
             weight_copy(direction, kk).start()
 
-    barrier = pltpu.get_barrier_semaphore()
-    for p in peers:
-        pl.semaphore_signal(barrier, inc=1, device_id={"dp": base + p}, device_id_type=MESH)
-
-    @pl.when(z > 0)
-    def _():
-        pl.semaphore_signal(barrier, inc=1, device_id={"head": z - 1}, device_id_type=MESH)
-
-    @pl.when(z < NZ - 1)
-    def _():
-        pl.semaphore_signal(barrier, inc=1, device_id={"head": z + 1}, device_id_type=MESH)
-
-    for h in range(2 * KVH):
-        block = query[0, :, h * HD:(h + 1) * HD].astype(F32)
-        squares = jnp.mean(block * block, axis=-1, keepdims=True)
-        normed = block * lax.rsqrt(squares + 1e-05) * qgain[...]
-        qall[g, 2 + h // 8, (h % 8) * 64:(h % 8 + 1) * 64, :] = normed.astype(BF16)
-    mall[g] = meta[...]
-
-    @pl.when(is_end)
-    def _():
-        pl.semaphore_wait(barrier, GROUP)
-
-    @pl.when(jnp.logical_not(is_end))
-    def _():
-        pl.semaphore_wait(barrier, GROUP + 1)
-
-    def q_up(dst_half, row):
-        return pltpu.make_async_remote_copy(
-            src_ref=qall.at[row, pl.ds(2, 2)], dst_ref=qall.at[row, pl.ds(dst_half, 2)],
-            send_sem=qzs, recv_sem=qzr, device_id={"head": beside}, device_id_type=MESH,
-        )
-
-    def q_forward(half, o, row):
-        return pltpu.make_async_remote_copy(
-            src_ref=qall.at[row, pl.ds(2 * half, 2)], dst_ref=qall.at[row, pl.ds(2 * half, 2)],
-            send_sem=qfs.at[half, o], recv_sem=qfr.at[half, o],
-            device_id={"dp": base + peers[o]}, device_id_type=MESH,
-        )
-
-    def meta_forward(o, row):
-        return pltpu.make_async_remote_copy(
-            src_ref=mall.at[row], dst_ref=mall.at[row], send_sem=ms.at[o], recv_sem=mr.at[o],
-            device_id={"dp": base + peers[o]}, device_id_type=MESH,
-        )
-
-    def part_send(kk, o, src_row, dst_row):
-        return pltpu.make_async_remote_copy(
-            src_ref=sbuf.at[kk, src_row], dst_ref=rbuf.at[kk, dst_row],
-            send_sem=ss.at[kk, o], recv_sem=sr.at[kk, o],
-            device_id={"dp": base + peers[o]}, device_id_type=MESH,
-        )
-
-    def out_send():
-        return pltpu.make_async_remote_copy(
-            src_ref=obuf.at[pl.ds(0, 2)], dst_ref=nbuf, send_sem=os_, recv_sem=or_,
-            device_id={"head": beside}, device_id_type=MESH,
-        )
-
-    @pl.when(jnp.logical_not(is_end))
-    def _():
-        q_up(0, g).start()
-
-    @pl.when(is_end)
-    def _():
-        for o in range(GROUP - 1):
-            meta_forward(o, g).start()
-            q_forward(1, o, g).start()
-
-    def chain(direction, i):
-        step = 1 if direction == 0 else -1
-        return pltpu.make_async_remote_copy(
-            src_ref=acc.at[direction, i], dst_ref=acc.at[direction, i],
-            send_sem=csend.at[direction, i], recv_sem=crecv.at[direction, i],
+    def send_queries():
+        for h in range(2 * KVH):
+            block = query[0, :, h * HD:(h + 1) * HD].astype(F32)
+            squares = jnp.mean(block * block, axis=-1, keepdims=True)
+            normed = block * lax.rsqrt(squares + 1e-05) * qgain[...]
+            qall[g, 2 + h // 8, (h % 8) * 64:(h % 8 + 1) * 64, :] = normed.astype(BF16)
+
+        @pl.when(jnp.logical_not(is_end))
+        def _():
+            q_up(0, g).start()
+
+        @pl.when(is_end)
+        def _():
+            for o in range(GROUP - 1):
+                meta_forward(o, g).start()
+                q_forward(1, o, g).start()
+
+    def chain(direction, i, half):
+        step = jnp.where(direction == 0, 1, -1)
+        rows = pl.ds(half * PIECE, PIECE)
+        return pltpu.make_async_remote_copy(
+            src_ref=acc.at[direction, i, rows], dst_ref=acc.at[direction, i, rows],
+            send_sem=csend.at[direction, half, i], recv_sem=crecv.at[direction, half, i],
             device_id={"head": z + step}, device_id_type=MESH,
         )
 
     def tail_chain(direction, kk):
-        step = 1 if direction == 0 else -1
+        step = jnp.where(direction == 0, 1, -1)
         return pltpu.make_async_remote_copy(
             src_ref=tacc.at[direction, kk], dst_ref=tacc.at[direction, kk],
             send_sem=tsend.at[direction, kk], recv_sem=trecv.at[direction, kk],
@@ -158,8 +174,8 @@
         )
 
     def add_link(direction, i):
-        first = (z == 0) if direction == 0 else (z == NZ - 1)
-        last = (z == NZ - 1) if direction == 0 else (z == 0)
+        first = z == jnp.where(direction == 0, 0, NZ - 1)
+        last = z == jnp.where(direction == 0, NZ - 1, 0)
         kk = i // UNIT
         c = lax.rem(i, UNIT)
 
@@ -182,18 +198,22 @@
 
         part = jnp.dot(fbuf[c], wbuf[direction, kk], preferred_element_type=F32)
 
-        @pl.when(first)
-        def _():
-            acc[direction, i] = part.astype(BF16)
-
-        @pl.when(jnp.logical_not(first))
-        def _():
-            chain(direction, i).wait_recv()
-            acc[direction, i] = (acc[direction, i].astype(F32) + part).astype(BF16)
-
-        @pl.when(jnp.logical_not(last))
-        def _():
-            chain(direction, i).start()
+        for half in range(HALVES):
+            rows = slice(half * PIECE, (half + 1) * PIECE)
+
+            @pl.when(first)
+            def _():
+                acc[direction, i, rows] = part[rows].astype(BF16)
+
+            @pl.when(jnp.logical_not(first))
+            def _():
+                chain(direction, i, half).wait_recv()
+                held_sum = acc[direction, i, rows].astype(F32)
+                acc[direction, i, rows] = (held_sum + part[rows]).astype(BF16)
+
+            @pl.when(jnp.logical_not(last))
+            def _():
+                chain(direction, i, half).start()
 
     def weigh(kv, s, valid):
         keys = kv[:, :HD]
@@ -294,19 +314,24 @@
                 for direction in range(2):
                     weight_copy(direction, kk).wait()
 
-        up = t - SKEW * z
-        down = t - SKEW * (NZ - 1 - z)
+        near_hop = jnp.where(is_end, 0, 1)
+        first_i = t - jnp.where(is_end, 0, AHEAD + 1)
+        other_i = t - (AHEAD + NZ - 1 - near_hop)
         d = t - LAST
 
-        @pl.when((up >= 0) & (up < STEPS))
-        def _():
-            add_link(0, up)
-
-        @pl.when((down >= 0) & (down < STEPS))
-        def _():
-            add_link(1, down)
-
-        @pl.when(is_end & (t == 1))
+        @pl.when((first_i >= 0) & (first_i < STEPS))
+        def _():
+            add_link(near, first_i)
+
+        @pl.when((other_i >= 0) & (other_i < STEPS))
+        def _():
+            add_link(1 - near, other_i)
+
+        @pl.when(t == 1)
+        def _():
+            send_queries()
+
+        @pl.when(is_end & (t == 3))
         def _():
             q_up(0, g).wait_recv()
             for o in range(GROUP - 1):
@@ -354,7 +379,8 @@
 
     def drain(direction):
         def each(i, carry):
-            chain(direction, i).wait_send()
+            for half in range(HALVES):
+                chain(direction, i, half).wait_send()
             return carry
 
         lax.fori_loop(0, STEPS, each, 0)
@@ -375,26 +401,17 @@
     tile_count, tile_slot, cross_mask, prompt_length,
 ):
     width = tile_features.shape[2]
-    prompt_rows = queries.shape[1]
     weight = projection.transpose(1, 0, 2)
-    tiles = jnp.arange(MAXT, dtype=jnp.int32)
-    rows = jnp.arange(prompt_rows, dtype=jnp.int32)
-    usable = (
-        (cross_mask[0].T == 1)
-        & (tiles[:, None] < tile_count[0])
-        & (rows[None, :] < prompt_length[0])
-    ).astype(jnp.int32)
-    usable = jnp.tile(usable, (1, HEADS // KVH))
-    held = jnp.where(tiles < tile_count[0], tile_slot[0], -1)
-    meta = jnp.concatenate([usable, jnp.broadcast_to(held[:, None], (MAXT, LANES))], axis=0)
+    mask = cross_mask.transpose(0, 2, 1)
 
     vmem = pl.BlockSpec(memory_space=pltpu.VMEM)
     hbm = pl.BlockSpec(memory_space=pl.ANY)
+    smem = pl.BlockSpec(memory_space=pltpu.SMEM)
     dma = pltpu.SemaphoreType.DMA
     return pl.pallas_call(
         kernel,
         out_shape=jax.ShapeDtypeStruct(queries.shape, BF16),
-        in_specs=[hbm, hbm, vmem, vmem, vmem, vmem],
+        in_specs=[smem, smem, smem, hbm, hbm, vmem, vmem, vmem, vmem],
         out_specs=vmem,
         scratch_shapes=[
             pltpu.VMEM((UNIT, ROWS, SLOTS_HERE, width), BF16),
@@ -417,8 +434,8 @@
             dma((UNIT,)),
             dma,
             dma((2, KHALF)),
-            dma((2, STEPS)),
-            dma((2, STEPS)),
+            dma((2, HALVES, STEPS)),
+            dma((2, HALVES, STEPS)),
             dma((2, KHALF)),
             dma((2, KHALF)),
             dma,
@@ -439,8 +456,8 @@
             flops=30_000_000_000, bytes_accessed=25_000_000, transcendentals=7_000_000
         ),
     )(
-        tile_features.transpose(1, 0, 2), weight, queries,
-        query_gain.reshape(1, HD), key_gain.reshape(1, HD), meta,
+        tile_count, tile_slot, prompt_length, tile_features.transpose(1, 0, 2), weight, queries,
+        query_gain.reshape(1, HD), key_gain.reshape(1, HD), mask,
     )
 
 

time: 196 us -> 186 us (0.949)
  Pallas kernels: 181 us -> 174 us
  other arithmetic: 2.1 us -> 0 us
    pallas_call x1, Pallas kernels: 181 us -> 174 us  [local(): pl.pallas_call(kernel, out_shape=jax.ShapeDtypeStruct(queries.shape, BF16...]
where the time goes in v3:
time: 186 us; the launch traced here: 185 us
  Pallas kernels  174 us (94%)
  local copies, waits for them, and re-layouts  9.61 us (5%)
    pallas_call x1, Pallas kernels, local(): pl.pallas_call(kernel, out_shape=jax.ShapeDtypeStruct(queries.shape, BF16...  174 us
    unnamed x2, local copies, waits for them, and re-layouts  9.61 us

profile of v3, /device:TPU:0, one launch (start us, length us, event | category | flops | bytes accessed | tf_op | source)
XLA Modules:
  0.0 184.8 jit_solution(12041962205594820840)
XLA Ops:
  1.3 7.9 %copy.12 = bf16[1920,8,256]{2,0,1:T(8,128)(2,1)} copy(bf16[1920,8,256]{2,1,0:T(8,128)(2,1)} %param.10) | data formatting | bytes 15728640 | tf_op args[1]
  9.2 173.9 %shard_map.91 = bf16[1,64,2048]{2,1,0:T(8,128)(2,1)} custom-call(s32[1]{0:T(128)S(6)} %copy.14.count, s32[1,4]{1,0:T(1,128)} %slots.1, s32[1]{0:T(128)S(6)} %copy.15.length, bf16[1601,2,1920]{2,1,0:T(2,128)(2,1)} %bitcast.8, bf16[8,1920,256]{2,1,0:T(8,128)(2,1)} %bitcast.7, bf16[1,64,2048]{2,1,0:T(8,128)(2,1)} %query.1, f32[1,128]{1,0:T(1,128)} %bitcast.10, ...), custom_call_target="tpu_custom_call" | custom-call | flops 30000001024 | bytes 25000000 | tf_op jit(solution)/shard_map/pallas_call | solution.py:411
  183.1 1.7 copy.16

commit v4 on v3

--- a/solution.py
+++ b/solution.py
@@ -18,7 +18,7 @@
 UNIT = 10
 LANES = 512
 AHEAD = 3
-HALVES = 2
+HALVES = 4
 LAG = 5
 KHALF = KVH // 2
 PAIRS = ROWS * SLOTS_HERE
@@ -179,23 +179,6 @@
         kk = i // UNIT
         c = lax.rem(i, UNIT)
 
-        @pl.when(lax.rem(i, UNIT) == 0)
-        def _():
-            part = jnp.dot(tail[...], wbuf[direction, kk], preferred_element_type=F32)
-
-            @pl.when(first)
-            def _():
-                tacc[direction, kk] = part.astype(BF16)
-
-            @pl.when(jnp.logical_not(first))
-            def _():
-                tail_chain(direction, kk).wait_recv()
-                tacc[direction, kk] = (tacc[direction, kk].astype(F32) + part).astype(BF16)
-
-            @pl.when(jnp.logical_not(last))
-            def _():
-                tail_chain(direction, kk).start()
-
         part = jnp.dot(fbuf[c], wbuf[direction, kk], preferred_element_type=F32)
 
         for half in range(HALVES):
@@ -214,6 +197,23 @@
             @pl.when(jnp.logical_not(last))
             def _():
                 chain(direction, i, half).start()
+
+        @pl.when(lax.rem(i, UNIT) == 0)
+        def _():
+            part = jnp.dot(tail[...], wbuf[direction, kk], preferred_element_type=F32)
+
+            @pl.when(first)
+            def _():
+                tacc[direction, kk] = part.astype(BF16)
+
+            @pl.when(jnp.logical_not(first))
+            def _():
+                tail_chain(direction, kk).wait_recv()
+                tacc[direction, kk] = (tacc[direction, kk].astype(F32) + part).astype(BF16)
+
+            @pl.when(jnp.logical_not(last))
+            def _():
+                tail_chain(direction, kk).start()
 
     def weigh(kv, s, valid):
         keys = kv[:, :HD]
@@ -267,7 +267,8 @@
         @pl.when(lax.rem(d, UNIT) == UNIT - 1)
         def _():
             row = lax.broadcasted_iota(jnp.int32, (16, LANES), 0)
-            for j in range(GROUP):
+            for o in (1, 0, 2, None):
+                j = g if o is None else peers[o]
                 total = jnp.zeros((HD, LANES), F32)
                 below = jnp.zeros((1, LANES), F32)
                 for s in range(SLOTS_HERE):
@@ -278,8 +279,8 @@
                 pair = jnp.where(row == 0, high, jnp.where(row == 1, below - high, 0.0))
                 sbuf[kk, j, :HD, :] = total.astype(BF16)
                 sbuf[kk, j, HD:, :] = pair.astype(BF16)
-            for o in range(GROUP - 1):
-                part_send(kk, o, peers[o], g).start()
+                if o is not None:
+                    part_send(kk, o, j, g).start()
 
     def finish(kk):
         for o in range(GROUP - 1):

time: 186 us -> 189 us (1.016)
  Pallas kernels: 174 us -> 178 us
    pallas_call x1, Pallas kernels: 174 us -> 178 us  [local(): pl.pallas_call(kernel, out_shape=jax.ShapeDtypeStruct(queries.shape, BF16...]
where the time goes in v4:
time: 189 us
  Pallas kernels  178 us (94%)
  local copies, waits for them, and re-layouts  9.61 us (5%)
    pallas_call x1, Pallas kernels, local(): pl.pallas_call(kernel, out_shape=jax.ShapeDtypeStruct(queries.shape, BF16...  178 us
    unnamed x2, local copies, waits for them, and re-layouts  9.61 us

profile of v4, /device:TPU:0, one launch (start us, length us, event | category | flops | bytes accessed | tf_op | source)
XLA Modules:
  0.0 188.8 jit_solution(4717047102646406790)
XLA Ops:
  1.3 7.9 %copy.12 = bf16[1920,8,256]{2,0,1:T(8,128)(2,1)} copy(bf16[1920,8,256]{2,1,0:T(8,128)(2,1)} %param.10) | data formatting | bytes 15728640 | tf_op args[1]
  9.2 177.9 %shard_map.91 = bf16[1,64,2048]{2,1,0:T(8,128)(2,1)} custom-call(s32[1]{0:T(128)S(6)} %copy.14.count, s32[1,4]{1,0:T(1,128)} %slots.1, s32[1]{0:T(128)S(6)} %copy.15.length, bf16[1601,2,1920]{2,1,0:T(2,128)(2,1)} %bitcast.8, bf16[8,1920,256]{2,1,0:T(8,128)(2,1)} %bitcast.7, bf16[1,64,2048]{2,1,0:T(8,128)(2,1)} %query.1, f32[1,128]{1,0:T(1,128)} %bitcast.10, ...), custom_call_target="tpu_custom_call" | custom-call | flops 30000001024 | bytes 25000000 | tf_op jit(solution)/shard_map/pallas_call | solution.py:412
  187.1 1.7 copy.16

commit v5 on v4

--- a/solution.py
+++ b/solution.py
@@ -18,7 +18,7 @@
 UNIT = 10
 LANES = 512
 AHEAD = 3
-HALVES = 4
+HALVES = 2
 LAG = 5
 KHALF = KVH // 2
 PAIRS = ROWS * SLOTS_HERE
@@ -36,7 +36,7 @@
 
 def kernel(
     count, slots, length, feat, weight, query, qgain, kgain, mask, out,
-    fraw, traw, fbuf, tail, kvf, wbuf, acc, tacc, qall, mall, qcur, num, den, sbuf, rbuf, obuf, nbuf,
+    fraw, traw, fbuf, tail, kvf, wbuf, acc, tacc, qall, mall, qcur, parts, num, den, sbuf, rbuf, obuf, nbuf,
     fsem, xsem, wsem, csend, crecv, tsend, trecv, qzs, qzr, qfs, qfr, ms, mr, ss, sr, os_, or_,
 ):
     dp = lax.axis_index("dp")
@@ -173,26 +173,28 @@
             device_id={"head": z + step}, device_id_type=MESH,
         )
 
-    def add_link(direction, i):
+    def multiply(place, direction, i):
+        parts[place] = jnp.dot(
+            fbuf[lax.rem(i, UNIT)], wbuf[direction, i // UNIT], preferred_element_type=F32
+        )
+
+    def add_link(place, direction, i):
         first = z == jnp.where(direction == 0, 0, NZ - 1)
         last = z == jnp.where(direction == 0, NZ - 1, 0)
         kk = i // UNIT
-        c = lax.rem(i, UNIT)
-
-        part = jnp.dot(fbuf[c], wbuf[direction, kk], preferred_element_type=F32)
 
         for half in range(HALVES):
             rows = slice(half * PIECE, (half + 1) * PIECE)
 
             @pl.when(first)
             def _():
-                acc[direction, i, rows] = part[rows].astype(BF16)
+                acc[direction, i, rows] = parts[place, rows].astype(BF16)
 
             @pl.when(jnp.logical_not(first))
             def _():
                 chain(direction, i, half).wait_recv()
                 held_sum = acc[direction, i, rows].astype(F32)
-                acc[direction, i, rows] = (held_sum + part[rows]).astype(BF16)
+                acc[direction, i, rows] = (held_sum + parts[place, rows]).astype(BF16)
 
             @pl.when(jnp.logical_not(last))
             def _():
@@ -298,7 +300,7 @@
         def _():
             out_send().start()
 
-    def body(t, carry):
+    def load(t):
         @pl.when(t < UNIT)
         def _():
             feat_copy(t).wait()
@@ -315,18 +317,35 @@
                 for direction in range(2):
                     weight_copy(direction, kk).wait()
 
+    def indices(t):
         near_hop = jnp.where(is_end, 0, 1)
         first_i = t - jnp.where(is_end, 0, AHEAD + 1)
         other_i = t - (AHEAD + NZ - 1 - near_hop)
+        return first_i, other_i
+
+    def prepare(t):
+        load(t)
+        first_i, other_i = indices(t)
+
+        @pl.when((first_i >= 0) & (first_i < STEPS))
+        def _():
+            multiply(0, near, first_i)
+
+        @pl.when((other_i >= 0) & (other_i < STEPS))
+        def _():
+            multiply(1, 1 - near, other_i)
+
+    def body(t, carry):
+        first_i, other_i = indices(t)
         d = t - LAST
 
         @pl.when((first_i >= 0) & (first_i < STEPS))
         def _():
-            add_link(near, first_i)
+            add_link(0, near, first_i)
 
         @pl.when((other_i >= 0) & (other_i < STEPS))
         def _():
-            add_link(1 - near, other_i)
+            add_link(1, 1 - near, other_i)
 
         @pl.when(t == 1)
         def _():
@@ -355,8 +374,10 @@
         def _():
             finish(late // UNIT)
 
+        prepare(t + 1)
         return carry
 
+    prepare(jnp.int32(0))
     lax.fori_loop(0, STEPS + LAST + LAG, body, 0)
 
     @pl.when(is_end)
@@ -426,6 +447,7 @@
             pltpu.VMEM((GROUP, KHALF, LANES, HD), BF16),
             pltpu.VMEM((GROUP, 2 * MAXT, LANES), jnp.int32),
             pltpu.VMEM((SLOTS_HERE, LANES, HD), BF16),
+            pltpu.VMEM((2, PAIRS, 2 * HD), F32),
             pltpu.VMEM((SLOTS_HERE, HD, LANES), F32),
             pltpu.VMEM((SLOTS_HERE, 1, LANES), F32),
             pltpu.VMEM((KHALF, GROUP, HD + 16, LANES), BF16),

time: 189 us -> 187 us (0.989)
  Pallas kernels: 178 us -> 176 us
    pallas_call x1, Pallas kernels: 178 us -> 176 us  [local(): pl.pallas_call(kernel, out_shape=jax.ShapeDtypeStruct(queries.shape, BF16...]
where the time goes in v5:
time: 187 us; the launch traced here: 186 us
  Pallas kernels  176 us (94%)
  local copies, waits for them, and re-layouts  9.61 us (5%)
    pallas_call x1, Pallas kernels, local(): pl.pallas_call(kernel, out_shape=jax.ShapeDtypeStruct(queries.shape, BF16...  176 us
    unnamed x2, local copies, waits for them, and re-layouts  9.61 us

profile of v5, /device:TPU:0, one launch (start us, length us, event | category | flops | bytes accessed | tf_op | source)
XLA Modules:
  0.0 186.4 jit_solution(12417397061346161492)
XLA Ops:
  1.3 7.9 %copy.12 = bf16[1920,8,256]{2,0,1:T(8,128)(2,1)} copy(bf16[1920,8,256]{2,1,0:T(8,128)(2,1)} %param.10) | data formatting | bytes 15728640 | tf_op args[1]
  9.2 175.5 %shard_map.91 = bf16[1,64,2048]{2,1,0:T(8,128)(2,1)} custom-call(s32[1]{0:T(128)S(6)} %copy.14.count, s32[1,4]{1,0:T(1,128)} %slots.1, s32[1]{0:T(128)S(6)} %copy.15.length, bf16[1601,2,1920]{2,1,0:T(2,128)(2,1)} %bitcast.8, bf16[8,1920,256]{2,1,0:T(8,128)(2,1)} %bitcast.7, bf16[1,64,2048]{2,1,0:T(8,128)(2,1)} %query.1, f32[1,128]{1,0:T(1,128)} %bitcast.10, ...), custom_call_target="tpu_custom_call" | custom-call | flops 30000001024 | bytes 25000000 | tf_op jit(solution)/shard_map/pallas_call | solution.py:433
  184.8 1.7 copy.16
